TPU v7x, 128 devices: a whole 4x4x4 slice. The times are simulated.
128 devices in a mesh: grp: 8 (over x, core), blk: 16 (over y, z).
Axes of the slice: x: 4, y: 4, z: 4, core: 2. Of those that a mesh axis runs over, the one named last changes fastest.
Arguments:
- stamps: float32 [128, 128, 64, 128], P(('grp', 'blk')), may hold values from -1 to 1
- stamp_target: int32 [128, 128, 128], P(('grp', 'blk')), may hold values from 0 to 4095
- pair_counts: int32 [128, 128], P(('grp', 'blk')), may hold values from 0 to 128, as said below
- conductance: float32 [8, 32768], P(None, ('grp', 'blk')), may hold values from 4 to 12
- block_cols: int32 [16, 32768], P(None, ('grp', 'blk')), may hold values from 0 to 32767, as said below
- newton_residual: float32 [8, 32768], P(None, ('grp', 'blk')), may hold values from -30 to 30
Outputs:
- update: float32 [8, 32768], P(None, ('grp', 'blk'))
- jacobian_blocks: float32 [16, 8, 8, 32768], P(None, None, None, ('grp', 'blk'))
- preconditioned_rhs: float32 [8, 32768], P(None, ('grp', 'blk'))
Inputs may be any that keep to these rules, and one draw needn't show every extreme that they name: `stamp_target`: A stamp's target is its block slot times 256 plus its block row local to the owner. `pair_counts`: every device sends exactly 128 live blocks to itself and exactly 128 to the next device in the order of grp+blk (the last device to the first), and at most 32 to every other owner; one owner drawn from the seed receives exactly 32 from every device other than itself and the device before it. `block_cols`: slot 0 of block row n names n itself; slots 1 to 7 name rows of the same group of 4096 rows as n; over the 256 block rows of one device, the slots from 8 on name rows owned by each device exactly 16 times.
All inputs are finite; a program needn't handle non-finite values.
Results may differ from a plain program's by a relative error of at most 0.0003.
Values sent between devices are 32-bit elements; how exact they have to be, the bound alone decides.
A program may use at most 128 MiB of HBM per device.

v0:
```python
import jax
import jax.numpy as jnp
from jax import lax
from jax.sharding import Mesh
from jax.sharding import PartitionSpec as P

K = 16
KRYLOV = 5
SWEEPS = 2
GRP = ("grp_0", "grp_1")
BLK = ("blk_0", "blk_1")
GRP_BLK = ("grp_0", "grp_1", "blk_0", "blk_1")
EPS = 1e-06


def sent_together(arrays, axis, split_dim, concat_dim, along):
    columns = [a.reshape(*a.shape[:along], -1) for a in arrays]
    both = jnp.concatenate(columns, axis=along)
    result, at, done = (
        lax.all_to_all(both, axis, split_axis=split_dim, concat_axis=concat_dim, tiled=True),
        0,
        [],
    )
    for a, column in zip(arrays, columns):
        piece = result[..., at : at + column.shape[along]]
        done.append(piece.reshape(*piece.shape[:along], *a.shape[along:]))
        at += column.shape[along]
    return tuple(done)


def passed_along(block, axis, distance):
    devices = range(lax.axis_size(axis))
    route = [((i - distance) % len(devices), i) for i in devices]
    return lax.ppermute(block, axis, route)


def in_order(parts, dim):
    dims = list(parts.shape[1:])
    dims[dim] *= parts.shape[0]
    return jnp.moveaxis(parts, 0, dim).reshape(dims)


def copy_for_each(array, axis):
    length = lax.axis_size(axis)
    return lax.all_to_all(
        jnp.broadcast_to(array[None], (length, *array.shape)), axis, 0, 0, tiled=True
    )


def collect(array, axis, dim):
    return in_order(copy_for_each(array, axis), dim)


def all_blocks(array, axes, sequence):
    parts = array[None]
    for k in sequence:
        parts = lax.all_gather(parts, axes[k], axis=0, tiled=True)
    held = [lax.axis_size(axes[k]) for k in reversed(sequence)]
    parts = parts.reshape(*held, *array.shape)
    turned = sorted(range(len(sequence)), key=lambda place: sequence[len(sequence) - 1 - place])
    return parts.transpose(*turned, *range(len(sequence), parts.ndim)).reshape(-1, *array.shape)


def gathered_by_axis(array, axes, sequence, dim):
    return in_order(all_blocks(array, axes, sequence), dim)


def by_axis(array, axes):
    for axis in axes:
        array = lax.psum(array, axis)
    return array


def invert_blocks(diag):
    size = diag.shape[0]
    eye_mat = jnp.eye(size, dtype=jnp.float32)[:, :, None]
    inverse = eye_mat * jnp.ones_like(diag[:1])
    work = diag
    for pivot_row in range(size):
        scale = 1.0 / work[pivot_row, pivot_row]
        top_work = work[pivot_row] * scale
        top_inverse = inverse[pivot_row] * scale
        factor = work[:, pivot_row]
        work = work - factor[:, None, :] * top_work[None]
        inverse = inverse - factor[:, None, :] * top_inverse[None]
        work = work.at[pivot_row].set(top_work)
        inverse = inverse.at[pivot_row].set(top_inverse)
    return inverse


def solve_small(matrix, rhs_vector):
    count = matrix.shape[0]
    work, vector = (matrix, rhs_vector)
    for pivot_row in range(count):
        scale = 1.0 / work[pivot_row, pivot_row]
        top_work = work[pivot_row] * scale
        top_rhs = vector[pivot_row] * scale
        factor = work[:, pivot_row]
        work = work - factor[:, None] * top_work[None, :]
        vector = vector - factor * top_rhs
        work = work.at[pivot_row].set(top_work)
        vector = vector.at[pivot_row].set(top_rhs)
    return vector


def block_apply(inverse, vector):
    return jnp.einsum("abn,bn->an", inverse, vector, precision=lax.Precision.HIGHEST)


def couple(jacobian, picked):
    return jnp.einsum("kabn,bkn->an", jacobian, picked, precision=lax.Precision.HIGHEST)


def add_stamps(summed, values, targets, counts, offset, local_rows):
    slots = values.shape[2]
    slot_ids = offset + jnp.arange(slots, dtype=jnp.int32)
    live = slot_ids[None, :] < counts
    masked = jnp.where(live[:, None, :], values, 0.0)
    index_pairs = jnp.stack([targets // local_rows, targets % local_rows], axis=2).astype(jnp.int32)
    numbers = lax.ScatterDimensionNumbers(
        update_window_dims=(1,), inserted_window_dims=(0, 2), scatter_dims_to_operand_dims=(0, 2)
    )
    return lax.scatter_add(summed, index_pairs, masked, numbers)


def local(stamps, stamp_target, pair_counts, conductance, block_cols, newton_residual):
    grp_count = lax.axis_size(GRP)
    blk_count = lax.axis_size(BLK)
    devices = grp_count * blk_count
    local_rows = conductance.shape[1]
    capacity = stamps.shape[3]
    summed = jnp.zeros((K, 64, local_rows), jnp.float32)
    front = capacity // 4
    got_values, got_target, got_counts = (
        lax.all_to_all(stamps[:, :, :, :front], GRP_BLK, split_axis=1, concat_axis=0, tiled=True),
        *sent_together((stamp_target[:, :, :front], pair_counts), GRP_BLK, 1, 0, 2),
    )
    summed = add_stamps(
        summed,
        got_values.reshape(devices, 64, front),
        got_target.reshape(devices, front),
        got_counts,
        0,
        local_rows,
    )
    my_index = lax.axis_index(GRP_BLK)
    next_index = (my_index + 1) % devices
    own_values = lax.dynamic_index_in_dim(stamps[0], my_index, 0, keepdims=False)[:, front:]
    own_target = lax.dynamic_index_in_dim(stamp_target[0], my_index, 0, keepdims=False)[front:]
    own_count = lax.dynamic_index_in_dim(pair_counts[0], my_index, 0, keepdims=True)
    next_values = lax.dynamic_index_in_dim(stamps[0], next_index, 0, keepdims=False)[:, front:]
    next_target = lax.dynamic_index_in_dim(stamp_target[0], next_index, 0, keepdims=False)[front:]
    next_count = lax.dynamic_index_in_dim(pair_counts[0], next_index, 0, keepdims=True)
    prior_values, prior_target, prior_count = passed_along(
        (next_values, next_target, next_count), GRP_BLK, 1
    )
    tail_values = jnp.stack([own_values, prior_values], axis=0)
    tail_target = jnp.stack([own_target, prior_target], axis=0)
    tail_counts = jnp.stack([own_count, prior_count], axis=0)
    summed = add_stamps(summed, tail_values, tail_target, tail_counts, front, local_rows)
    jacobian = summed.reshape(K, 8, 8, local_rows)
    identity = jnp.eye(8, dtype=jnp.float32)
    jacobian = jacobian.at[0].add(identity[:, :, None] * conductance[:, None, :])
    inverse = invert_blocks(jacobian[0])
    group_rows = local_rows * blk_count
    group_start = lax.axis_index(GRP) * group_rows
    slot_ids = jnp.arange(K, dtype=jnp.int32)[:, None]
    near = (block_cols >= group_start) & (block_cols < group_start + group_rows) & (slot_ids >= 1)
    local_cols = jnp.clip(block_cols - group_start, 0, group_rows - 1)
    rhs_field = -newton_residual
    beta = jnp.sqrt(by_axis(jnp.sum(rhs_field * rhs_field), GRP_BLK) + EPS)
    basis = [rhs_field / beta]
    search = []
    hess = jnp.zeros((KRYLOV + 1, KRYLOV), jnp.float32)
    for krylov_step in range(KRYLOV):
        precondition_vector = basis[krylov_step]
        result = block_apply(inverse, precondition_vector)
        for sweep_index in range(SWEEPS):
            grouped = collect(result, BLK, 1)
            precondition_picked = jnp.where(near[None], grouped[:, local_cols], 0.0)
            result = block_apply(
                inverse, precondition_vector - couple(jacobian, precondition_picked)
            )
        search.append(result)
        whole = gathered_by_axis(result, GRP_BLK, (0, 2, 3, 1), 1)
        picked = whole[:, block_cols]
        image = couple(jacobian, picked)
        partial_value = jnp.stack([jnp.sum(basis_vec * image) for basis_vec in basis])
        projections, squares = (
            by_axis(partial_value, GRP_BLK),
            by_axis(jnp.sum(image * image), GRP_BLK),
        )
        for index_i, basis_vec in enumerate(basis):
            image = image - projections[index_i] * basis_vec
        length = jnp.sqrt(squares - jnp.sum(projections * projections) + EPS)
        hess = hess.at[: krylov_step + 1, krylov_step].set(projections)
        hess = hess.at[krylov_step + 1, krylov_step].set(length)
        if krylov_step + 1 < KRYLOV:
            basis.append(image / length)
    normal = jnp.dot(hess.T, hess, precision=lax.Precision.HIGHEST)
    coef = solve_small(normal, beta * hess[0])
    update = coef[0] * search[0]
    for index_j in range(1, KRYLOV):
        update = update + coef[index_j] * search[index_j]
    return (update, jacobian, beta * search[0])


def solution(mesh):
    torus = Mesh(mesh.devices.reshape(4, 2, 4, 4), ("grp_0", "grp_1", "blk_0", "blk_1"))
    return jax.shard_map(
        local,
        mesh=torus,
        in_specs=(
            P(GRP_BLK, None, None, None),
            P(GRP_BLK, None, None),
            P(GRP_BLK, None),
            P(None, GRP_BLK),
            P(None, GRP_BLK),
            P(None, GRP_BLK),
        ),
        out_specs=(P(None, GRP_BLK), P(None, None, None, GRP_BLK), P(None, GRP_BLK)),
        check_vma=False,
    )
```

profile of v0, /device:TPU:2, one launch (start us, length us, event | category | flops | bytes accessed | tf_op | source)
XLA Modules:
  0.0 1031.7 jit_solution(8667777961732287962)
XLA Ops:
  56.9 11.8 %psum.311 = f32[]{:T(128)} all-reduce(f32[]{:T(128)} %psum.310), channel_id=1, replica_groups=mesh['grp_0'=4,'grp_1'=2,'blk_0'=4,'blk_1'=4] {'blk_1'}, use_global_device_ids=true, to_apply=%region_4.5 | all-reduce | flops 1 | bytes 8 | tf_op jit(solution)/shard_map/psum | solution.py:70
  77.9 17.9 %all-to-all-done.1 = f32[128,1,2048]{2,1,0:T(1,128)S(1)} async-done(((f32[128,1,2048]{2,1,0:T(1,128)}), f32[128,1,2048]{2,1,0:T(1,128)S(1)}, u32[]{:S(2)}, u32[]{:S(2)}) %all-to-all-start.1) | async-done | bytes 1048608 | tf_op jit(solution)/shard_map/all_to_all | solution.py:135
  102.8 23.6 %scatter_custom_fusion.1 = f32[4096,64]{1,0:T(8,128)S(1)} fusion(s32[4096]{0:T(1024)S(1)} %reshape.1985, f32[4096,64]{1,0:T(8,128)} %bitcast.629, f32[]{:T(128)} %constant.944.clone.1), kind=kCustom, calls=%fused_computation.43 | custom fusion | flops 262144 | bytes 1049088
  150.7 14.1 %gather_fusion = f32[4096,8]{1,0:T(8,128)} fusion(f32[8,4096]{0,1:T(8,128)S(1)} %bitcast.604, s32[4096]{0:T(1024)S(1)} %broadcast_clamp_fusion.1), kind=kCustom, calls=%fused_computation | custom fusion | bytes 278528 | tf_op jit(solution)/shard_map/gather | solution.py:180
  167.5 11.3 %all_to_all.71 = f32[16,8,256]{2,1,0:T(8,128)S(1)} all-to-all(f32[16,8,256]{2,1,0:T(8,128)S(1)} %broadcast_in_dim.117), channel_id=1, replica_groups=mesh['grp_0'=4,'grp_1'=2,'blk_0'=4,'blk_1'=4] {'blk_0','blk_1'}, dimensions={0} | all-to-all | bytes 262144 | tf_op jit(solution)/shard_map/all_to_all | solution.py:45
  179.4 14.1 %gather_fusion.1 = f32[4096,8]{1,0:T(8,128)} fusion(f32[8,4096]{0,1:T(8,128)S(1)} %bitcast.605, s32[4096]{0:T(1024)S(1)} %broadcast_clamp_fusion.1), kind=kCustom, calls=%fused_computation.1 | custom fusion | bytes 278528 | tf_op jit(solution)/shard_map/gather | solution.py:180
  196.1 11.3 %all-gather = f32[32,256]{1,0:T(8,128)S(1)} all-gather(f32[8,256]{1,0:T(8,128)S(1)} %bitcast.658), channel_id=2, replica_groups=mesh['grp_0'=4,'grp_1'=2,'blk_0'=4,'blk_1'=4] {'grp_0'}, dimensions={0}, use_global_device_ids=true | all-gather | bytes 40960 | tf_op jit(solution)/shard_map/all_gather | solution.py:57
  207.4 12.0 %all_gather.61 = f32[16,8,256]{2,1,0:T(8,128)S(1)} all-gather(f32[4,8,256]{2,1,0:T(8,128)S(1)} %bitcast.653), channel_id=1, replica_groups=mesh['grp_0'=4,'grp_1'=2,'blk_0'=4,'blk_1'=4] {'blk_0'}, dimensions={0}, use_global_device_ids=true | all-gather | bytes 163840 | tf_op jit(solution)/shard_map/all_gather | solution.py:57
  219.4 13.5 %all_gather.62 = f32[64,8,256]{2,1,0:T(8,128)} all-gather(f32[16,8,256]{2,1,0:T(8,128)S(1)} %all_gather.61), channel_id=1, replica_groups=mesh['grp_0'=4,'grp_1'=2,'blk_0'=4,'blk_1'=4] {'blk_1'}, dimensions={0}, use_global_device_ids=true | all-gather | bytes 655360 | tf_op jit(solution)/shard_map/all_gather | solution.py:57
  252.6 16.5 %gather_fusion.2 = f32[4096,8]{1,0:T(8,128)S(1)} fusion(f32[8,32768]{0,1:T(8,128)} %bitcast.597, s32[4096]{0:T(1024)S(1)} %broadcast_clamp_fusion), kind=kCustom, calls=%fused_computation.2 | custom fusion | bytes 278528 | tf_op jit(solution)/shard_map/gather | solution.py:186
  282.7 11.1 %all-reduce.10 = (f32[1]{0:T(128)}, f32[]{:T(128)}) all-reduce(f32[1]{0:T(128)} %get-tuple-element.481, f32[]{:T(128)} %get-tuple-element.482), channel_id=1, replica_groups=mesh['grp_0'=4,'grp_1'=2,'blk_0'=4,'blk_1'=4] {'blk_0'}, use_global_device_ids=true, to_apply=%region_10.11 | all-reduce | flops 2 | bytes 16 | tf_op jit(solution)/shard_map/psum | solution.py:70
  293.8 11.3 %all-reduce.5 = (f32[1]{0:T(128)}, f32[]{:T(128)}) all-reduce(f32[1]{0:T(128)} %get-tuple-element.461, f32[]{:T(128)} %get-tuple-element.462), channel_id=1, replica_groups=mesh['grp_0'=4,'grp_1'=2,'blk_0'=4,'blk_1'=4] {'blk_1'}, use_global_device_ids=true, to_apply=%region_11.12 | all-reduce | flops 2 | bytes 16 | tf_op jit(solution)/shard_map/psum | solution.py:70
  318.8 14.1 %gather_fusion.3 = f32[4096,8]{1,0:T(8,128)} fusion(f32[8,4096]{0,1:T(8,128)S(1)} %bitcast.606, s32[4096]{0:T(1024)S(1)} %broadcast_clamp_fusion.1), kind=kCustom, calls=%fused_computation.3 | custom fusion | bytes 278528 | tf_op jit(solution)/shard_map/gather | solution.py:180
  335.6 11.3 %all_to_all.73 = f32[16,8,256]{2,1,0:T(8,128)S(1)} all-to-all(f32[16,8,256]{2,1,0:T(8,128)S(1)} %broadcast_in_dim.121), channel_id=1, replica_groups=mesh['grp_0'=4,'grp_1'=2,'blk_0'=4,'blk_1'=4] {'blk_0','blk_1'}, dimensions={0} | all-to-all | bytes 262144 | tf_op jit(solution)/shard_map/all_to_all | solution.py:45
  347.5 14.1 %gather_fusion.4 = f32[4096,8]{1,0:T(8,128)} fusion(f32[8,4096]{0,1:T(8,128)S(1)} %bitcast.607, s32[4096]{0:T(1024)S(1)} %broadcast_clamp_fusion.1), kind=kCustom, calls=%fused_computation.4 | custom fusion | bytes 278528 | tf_op jit(solution)/shard_map/gather | solution.py:180
  364.2 11.1 %all-gather.1 = f32[32,256]{1,0:T(8,128)S(1)} all-gather(f32[8,256]{1,0:T(8,128)S(1)} %bitcast.659), channel_id=3, replica_groups=mesh['grp_0'=4,'grp_1'=2,'blk_0'=4,'blk_1'=4] {'grp_0'}, dimensions={0}, use_global_device_ids=true | all-gather | bytes 40960 | tf_op jit(solution)/shard_map/all_gather | solution.py:57
  375.3 12.0 %all_gather.65 = f32[16,8,256]{2,1,0:T(8,128)S(1)} all-gather(f32[4,8,256]{2,1,0:T(8,128)S(1)} %bitcast.654), channel_id=1, replica_groups=mesh['grp_0'=4,'grp_1'=2,'blk_0'=4,'blk_1'=4] {'blk_0'}, dimensions={0}, use_global_device_ids=true | all-gather | bytes 163840 | tf_op jit(solution)/shard_map/all_gather | solution.py:57
  387.3 13.5 %all_gather.66 = f32[64,8,256]{2,1,0:T(8,128)} all-gather(f32[16,8,256]{2,1,0:T(8,128)S(1)} %all_gather.65), channel_id=1, replica_groups=mesh['grp_0'=4,'grp_1'=2,'blk_0'=4,'blk_1'=4] {'blk_1'}, dimensions={0}, use_global_device_ids=true | all-gather | bytes 655360 | tf_op jit(solution)/shard_map/all_gather | solution.py:57
  400.9 11.1 %all-gather.13.cloned.1.call-done = f32[128,8,256]{2,1,0:T(8,128)} async-done(((f32[64,8,256]{2,1,0:T(8,128)}), f32[128,8,256]{2,1,0:T(8,128)}) %all-gather.13.cloned.1.call-update) | async-done | bytes 1048592 | tf_op jit(solution)/shard_map/all_gather | solution.py:57
  421.8 16.5 %gather_fusion.5 = f32[4096,8]{1,0:T(8,128)S(1)} fusion(f32[8,32768]{0,1:T(8,128)} %bitcast.598, s32[4096]{0:T(1024)S(1)} %broadcast_clamp_fusion), kind=kCustom, calls=%fused_computation.5 | custom fusion | bytes 278528 | tf_op jit(solution)/shard_map/gather | solution.py:186
  453.3 11.1 %all-reduce.9 = (f32[2]{0:T(128)S(1)}, f32[]{:T(128)}) all-reduce(f32[2]{0:T(128)S(1)} %get-tuple-element.479, f32[]{:T(128)} %get-tuple-element.480), channel_id=1, replica_groups=mesh['grp_0'=4,'grp_1'=2,'blk_0'=4,'blk_1'=4] {'blk_0'}, use_global_device_ids=true, to_apply=%region_22.23 | all-reduce | flops 3 | bytes 24 | tf_op jit(solution)/shard_map/psum | solution.py:70
  464.4 11.4 %all-reduce.4 = (f32[2]{0:T(128)S(1)}, f32[]{:T(128)}) all-reduce(f32[2]{0:T(128)S(1)} %get-tuple-element.459, f32[]{:T(128)} %get-tuple-element.460), channel_id=1, replica_groups=mesh['grp_0'=4,'grp_1'=2,'blk_0'=4,'blk_1'=4] {'blk_1'}, use_global_device_ids=true, to_apply=%region_23.24 | all-reduce | flops 3 | bytes 24 | tf_op jit(solution)/shard_map/psum | solution.py:70
  490.8 14.1 %gather_fusion.6 = f32[4096,8]{1,0:T(8,128)} fusion(f32[8,4096]{0,1:T(8,128)S(1)} %bitcast.608, s32[4096]{0:T(1024)S(1)} %broadcast_clamp_fusion.1), kind=kCustom, calls=%fused_computation.6 | custom fusion | bytes 278528 | tf_op jit(solution)/shard_map/gather | solution.py:180
  507.6 11.3 %all_to_all.75 = f32[16,8,256]{2,1,0:T(8,128)S(1)} all-to-all(f32[16,8,256]{2,1,0:T(8,128)S(1)} %broadcast_in_dim.124), channel_id=1, replica_groups=mesh['grp_0'=4,'grp_1'=2,'blk_0'=4,'blk_1'=4] {'blk_0','blk_1'}, dimensions={0} | all-to-all | bytes 262144 | tf_op jit(solution)/shard_map/all_to_all | solution.py:45
  519.5 14.1 %gather_fusion.7 = f32[4096,8]{1,0:T(8,128)} fusion(f32[8,4096]{0,1:T(8,128)S(1)} %bitcast.609, s32[4096]{0:T(1024)S(1)} %broadcast_clamp_fusion.1), kind=kCustom, calls=%fused_computation.7 | custom fusion | bytes 278528 | tf_op jit(solution)/shard_map/gather | solution.py:180
  536.2 11.1 %all-gather.2 = f32[32,256]{1,0:T(8,128)S(1)} all-gather(f32[8,256]{1,0:T(8,128)S(1)} %bitcast.660), channel_id=4, replica_groups=mesh['grp_0'=4,'grp_1'=2,'blk_0'=4,'blk_1'=4] {'grp_0'}, dimensions={0}, use_global_device_ids=true | all-gather | bytes 40960 | tf_op jit(solution)/shard_map/all_gather | solution.py:57
  547.3 12.0 %all_gather.69 = f32[16,8,256]{2,1,0:T(8,128)S(1)} all-gather(f32[4,8,256]{2,1,0:T(8,128)S(1)} %bitcast.655), channel_id=1, replica_groups=mesh['grp_0'=4,'grp_1'=2,'blk_0'=4,'blk_1'=4] {'blk_0'}, dimensions={0}, use_global_device_ids=true | all-gather | bytes 163840 | tf_op jit(solution)/shard_map/all_gather | solution.py:57
  559.3 13.5 %all_gather.70 = f32[64,8,256]{2,1,0:T(8,128)} all-gather(f32[16,8,256]{2,1,0:T(8,128)S(1)} %all_gather.69), channel_id=1, replica_groups=mesh['grp_0'=4,'grp_1'=2,'blk_0'=4,'blk_1'=4] {'blk_1'}, dimensions={0}, use_global_device_ids=true | all-gather | bytes 655360 | tf_op jit(solution)/shard_map/all_gather | solution.py:57
  572.9 11.1 %all-gather.15.cloned.1.call-done = f32[128,8,256]{2,1,0:T(8,128)} async-done(((f32[64,8,256]{2,1,0:T(8,128)}), f32[128,8,256]{2,1,0:T(8,128)}) %all-gather.15.cloned.1.call-update) | async-done | bytes 1048592 | tf_op jit(solution)/shard_map/all_gather | solution.py:57
  593.8 16.5 %gather_fusion.8 = f32[4096,8]{1,0:T(8,128)S(1)} fusion(f32[8,32768]{0,1:T(8,128)} %bitcast.599, s32[4096]{0:T(1024)S(1)} %broadcast_clamp_fusion), kind=kCustom, calls=%fused_computation.8 | custom fusion | bytes 278528 | tf_op jit(solution)/shard_map/gather | solution.py:186
  625.9 11.1 %all-reduce.8 = (f32[3]{0:T(128)S(1)}, f32[]{:T(128)}) all-reduce(f32[3]{0:T(128)S(1)} %get-tuple-element.477, f32[]{:T(128)} %get-tuple-element.478), channel_id=1, replica_groups=mesh['grp_0'=4,'grp_1'=2,'blk_0'=4,'blk_1'=4] {'blk_0'}, use_global_device_ids=true, to_apply=%region_36.37 | all-reduce | flops 4 | bytes 32 | tf_op jit(solution)/shard_map/psum | solution.py:70
  637.0 11.4 %all-reduce.3 = (f32[3]{0:T(128)S(1)}, f32[]{:T(128)}) all-reduce(f32[3]{0:T(128)S(1)} %get-tuple-element.457, f32[]{:T(128)} %get-tuple-element.458), channel_id=1, replica_groups=mesh['grp_0'=4,'grp_1'=2,'blk_0'=4,'blk_1'=4] {'blk_1'}, use_global_device_ids=true, to_apply=%region_37.38 | all-reduce | flops 4 | bytes 32 | tf_op jit(solution)/shard_map/psum | solution.py:70
  663.9 14.1 %gather_fusion.9 = f32[4096,8]{1,0:T(8,128)} fusion(f32[8,4096]{0,1:T(8,128)S(1)} %bitcast.610, s32[4096]{0:T(1024)S(1)} %broadcast_clamp_fusion.1), kind=kCustom, calls=%fused_computation.9 | custom fusion | bytes 278528 | tf_op jit(solution)/shard_map/gather | solution.py:180
  680.7 11.3 %all_to_all.77 = f32[16,8,256]{2,1,0:T(8,128)S(1)} all-to-all(f32[16,8,256]{2,1,0:T(8,128)S(1)} %broadcast_in_dim.127), channel_id=1, replica_groups=mesh['grp_0'=4,'grp_1'=2,'blk_0'=4,'blk_1'=4] {'blk_0','blk_1'}, dimensions={0} | all-to-all | bytes 262144 | tf_op jit(solution)/shard_map/all_to_all | solution.py:45
  692.5 14.1 %gather_fusion.10 = f32[4096,8]{1,0:T(8,128)} fusion(f32[8,4096]{0,1:T(8,128)S(1)} %bitcast.611, s32[4096]{0:T(1024)S(1)} %broadcast_clamp_fusion.1), kind=kCustom, calls=%fused_computation.10 | custom fusion | bytes 278528 | tf_op jit(solution)/shard_map/gather | solution.py:180
  709.3 11.1 %all-gather.3 = f32[32,256]{1,0:T(8,128)S(1)} all-gather(f32[8,256]{1,0:T(8,128)S(1)} %bitcast.661), channel_id=5, replica_groups=mesh['grp_0'=4,'grp_1'=2,'blk_0'=4,'blk_1'=4] {'grp_0'}, dimensions={0}, use_global_device_ids=true | all-gather | bytes 40960 | tf_op jit(solution)/shard_map/all_gather | solution.py:57
  720.4 12.0 %all_gather.73 = f32[16,8,256]{2,1,0:T(8,128)S(1)} all-gather(f32[4,8,256]{2,1,0:T(8,128)S(1)} %bitcast.656), channel_id=1, replica_groups=mesh['grp_0'=4,'grp_1'=2,'blk_0'=4,'blk_1'=4] {'blk_0'}, dimensions={0}, use_global_device_ids=true | all-gather | bytes 163840 | tf_op jit(solution)/shard_map/all_gather | solution.py:57
  732.3 13.5 %all_gather.74 = f32[64,8,256]{2,1,0:T(8,128)} all-gather(f32[16,8,256]{2,1,0:T(8,128)S(1)} %all_gather.73), channel_id=1, replica_groups=mesh['grp_0'=4,'grp_1'=2,'blk_0'=4,'blk_1'=4] {'blk_1'}, dimensions={0}, use_global_device_ids=true | all-gather | bytes 655360 | tf_op jit(solution)/shard_map/all_gather | solution.py:57
  766.8 16.5 %gather_fusion.11 = f32[4096,8]{1,0:T(8,128)S(1)} fusion(f32[8,32768]{0,1:T(8,128)} %bitcast.600, s32[4096]{0:T(1024)S(1)} %broadcast_clamp_fusion), kind=kCustom, calls=%fused_computation.11 | custom fusion | bytes 278528 | tf_op jit(solution)/shard_map/gather | solution.py:186
  799.6 11.1 %all-reduce.7 = (f32[4]{0:T(128)S(1)}, f32[]{:T(128)}) all-reduce(f32[4]{0:T(128)S(1)} %get-tuple-element.475, f32[]{:T(128)} %get-tuple-element.476), channel_id=1, replica_groups=mesh['grp_0'=4,'grp_1'=2,'blk_0'=4,'blk_1'=4] {'blk_0'}, use_global_device_ids=true, to_apply=%region_51.52 | all-reduce | flops 5 | bytes 40 | tf_op jit(solution)/shard_map/psum | solution.py:70
  810.7 11.3 %all-reduce.2 = (f32[4]{0:T(128)S(1)}, f32[]{:T(128)}) all-reduce(f32[4]{0:T(128)S(1)} %get-tuple-element.455, f32[]{:T(128)} %get-tuple-element.456), channel_id=1, replica_groups=mesh['grp_0'=4,'grp_1'=2,'blk_0'=4,'blk_1'=4] {'blk_1'}, use_global_device_ids=true, to_apply=%region_52.53 | all-reduce | flops 5 | bytes 40 | tf_op jit(solution)/shard_map/psum | solution.py:70
  839.6 14.1 %gather_fusion.12 = f32[4096,8]{1,0:T(8,128)} fusion(f32[8,4096]{0,1:T(8,128)S(1)} %bitcast.612, s32[4096]{0:T(1024)S(1)} %broadcast_clamp_fusion.1), kind=kCustom, calls=%fused_computation.12 | custom fusion | bytes 278528 | tf_op jit(solution)/shard_map/gather | solution.py:180
  869.1 14.1 %gather_fusion.13 = f32[4096,8]{1,0:T(8,128)} fusion(f32[8,4096]{0,1:T(8,128)S(1)} %bitcast.603, s32[4096]{0:T(1024)S(1)} %broadcast_clamp_fusion.1), kind=kCustom, calls=%fused_computation.13 | custom fusion | bytes 278528 | tf_op jit(solution)/shard_map/gather | solution.py:180
  885.9 11.1 %all-gather.4 = f32[32,256]{1,0:T(8,128)S(1)} all-gather(f32[8,256]{1,0:T(8,128)S(1)} %bitcast.662), channel_id=6, replica_groups=mesh['grp_0'=4,'grp_1'=2,'blk_0'=4,'blk_1'=4] {'grp_0'}, dimensions={0}, use_global_device_ids=true | all-gather | bytes 40960 | tf_op jit(solution)/shard_map/all_gather | solution.py:57
  897.0 12.0 %all_gather.77 = f32[16,8,256]{2,1,0:T(8,128)S(1)} all-gather(f32[4,8,256]{2,1,0:T(8,128)S(1)} %bitcast.657), channel_id=1, replica_groups=mesh['grp_0'=4,'grp_1'=2,'blk_0'=4,'blk_1'=4] {'blk_0'}, dimensions={0}, use_global_device_ids=true | all-gather | bytes 163840 | tf_op jit(solution)/shard_map/all_gather | solution.py:57
  909.0 13.5 %all_gather.78 = f32[64,8,256]{2,1,0:T(8,128)} all-gather(f32[16,8,256]{2,1,0:T(8,128)S(1)} %all_gather.77), channel_id=1, replica_groups=mesh['grp_0'=4,'grp_1'=2,'blk_0'=4,'blk_1'=4] {'blk_1'}, dimensions={0}, use_global_device_ids=true | all-gather | bytes 655360 | tf_op jit(solution)/shard_map/all_gather | solution.py:57
  947.0 16.5 %gather_fusion.14 = f32[4096,8]{1,0:T(8,128)S(1)} fusion(f32[8,32768]{0,1:T(8,128)} %bitcast.596, s32[4096]{0:T(1024)S(1)} %broadcast_clamp_fusion), kind=kCustom, calls=%fused_computation.14 | custom fusion | bytes 278528 | tf_op jit(solution)/shard_map/gather | solution.py:186
  968.1 11.6 %all-reduce.11 = (f32[5]{0:T(128)S(1)}, f32[]{:T(128)}) all-reduce(f32[5]{0:T(128)S(1)} %stack.120, f32[]{:T(128)} %get-tuple-element.423), channel_id=1, replica_groups=mesh['grp_0'=4,'grp_1'=2,'blk_0'=4,'blk_1'=4] {'grp_0'}, use_global_device_ids=true, to_apply=%region_65.66 | all-reduce | flops 6 | bytes 48 | tf_op jit(solution)/shard_map/psum | solution.py:70
  (336 shorter events, 373.2 us)
Async XLA Ops:
  8.5 60.9 %collective-permute-start.1 = (s32[1]{0:T(128)}, s32[1]{0:T(128)}, u32[]{:S(2)}, u32[]{:S(2)}) collective-permute-start(s32[1]{0:T(128)} %bitcast.71), channel_id=1, source_target_pairs={{127,0},{0,1},{1,2},{2,3},{3,4},{4,5},{5,6},{6,7},{7,8},{8,9},{9,1... | collective-permute-start | bytes 20 | tf_op jit(solution)/shard_map/ppermute | solution.py:34
  11.3 66.4 %collective-permute-start.2 = (f32[64,96]{1,0:T(8,128)S(1)}, f32[64,96]{1,0:T(8,128)S(1)}, u32[]{:S(2)}, u32[]{:S(2)}) collective-permute-start(f32[64,96]{1,0:T(8,128)S(1)} %slice.984), channel_id=1, source_target_pairs={{127,0},{0,1},{1,2},{2,3},{3,4},{4,5},{5,6},{6,7},{7,8},{8,9},{9,1... | collective-permute-start | bytes 73736 | tf_op jit(solution)/shard_map/ppermute | solution.py:34
  14.1 56.9 %collective-permute-start = (s32[96]{0:T(128)S(1)}, s32[96]{0:T(128)S(1)}, u32[]{:S(2)}, u32[]{:S(2)}) collective-permute-start(s32[96]{0:T(128)S(1)} %slice_bitcast_fusion.6), channel_id=1, source_target_pairs={{127,0},{0,1},{1,2},{2,3},{3,4},{4,5},{5,6},{6,7},{7,8},{8,9},{9,1... | collective-permute-start | bytes 1160 | tf_op jit(solution)/shard_map/ppermute | solution.py:34
  18.0 53.0 %all-to-all-start = ((s32[1,128,33]{2,0,1:T(1,128)}), s32[1,128,33]{2,0,1:T(1,128)S(1)}, u32[]{:S(2)}, u32[]{:S(2)}) async-start(s32[1,128,33]{2,0,1:T(1,128)} %copy.71), calls=%async_computation | async-start | bytes 131072 | tf_op jit(solution)/shard_map/all_to_all | solution.py:20
  43.6 25.7 %copy-start.1 = (f32[8,256]{1,0:T(8,128)S(1)}, f32[8,256]{1,0:T(8,128)}, u32[]{:S(2)}) copy-start(f32[8,256]{1,0:T(8,128)} %param.81) | copy-start | bytes 24580
  43.6 25.8 %copy-start.3 = (s32[16,256]{1,0:T(8,128)S(1)}, s32[16,256]{1,0:T(8,128)}, u32[]{:S(2)}) copy-start(s32[16,256]{1,0:T(8,128)} %param.80) | copy-start | bytes 49156
  56.8 20.3 %copy-start.5 = (s32[2]{0:T(128)S(1)}, s32[2]{0:T(128)}, u32[]{:S(2)}) copy-start(s32[2]{0:T(128)} %constant.981) | copy-start | bytes 28
  56.8 20.4 %copy-start.4 = (s32[2]{0:T(128)S(1)}, s32[2]{0:T(128)}, u32[]{:S(2)}) copy-start(s32[2]{0:T(128)} %constant.984) | copy-start | bytes 28
  71.1 24.8 %all-to-all-start.1 = ((f32[128,1,2048]{2,1,0:T(1,128)}), f32[128,1,2048]{2,1,0:T(1,128)S(1)}, u32[]{:S(2)}, u32[]{:S(2)}) async-start(f32[128,1,2048]{2,1,0:T(1,128)} %reshape.2102), calls=%async_computation.1 | async-start | bytes 2097152 | tf_op jit(solution)/shard_map/all_to_all | solution.py:135
  136.3 0.7 copy-start.2
  137.2 826.8 %copy-start = (f32[16,8,8,256]{3,2,1,0:T(8,128)}, f32[16,8,8,256]{3,2,1,0:T(8,128)S(1)}, u32[]{:S(2)}) copy-start(f32[16,8,8,256]{3,2,1,0:T(8,128)S(1)} %get-tuple-element.493) | copy-start | bytes 3145732
  138.8 11.3 %all-to-all-start.2 = ((f32[16,8,256]{2,1,0:T(8,128)}), f32[16,8,256]{2,1,0:T(8,128)S(1)}, u32[]{:S(2)}, u32[]{:S(2)}) async-start(f32[16,8,256]{2,1,0:T(8,128)} %broadcast_in_dim.114), calls=%async_computation.2 | async-start | bytes 262144 | tf_op jit(solution)/shard_map/all_to_all | solution.py:45
  142.3 100.5 %all-gather.11.cloned.1.call-start = ((), (), s32[]{:S(2)}) async-start(), calls=%async_computation.12 | async-start | bytes 1572864 | tf_op jit(solution)/shard_map/all_gather | solution.py:57
  232.9 179.0 %all-gather.13.cloned.1.call-start = ((), (), s32[]{:S(2)}) async-start(), calls=%async_computation.13 | async-start | bytes 1572864 | tf_op jit(solution)/shard_map/all_gather | solution.py:57
  400.8 183.1 %all-gather.15.cloned.1.call-start = ((), (), s32[]{:S(2)}) async-start(), calls=%async_computation.14 | async-start | bytes 1572864 | tf_op jit(solution)/shard_map/all_gather | solution.py:57
  572.8 184.2 %all-gather.17.cloned.1.call-start = ((), (), s32[]{:S(2)}) async-start(), calls=%async_computation.15 | async-start | bytes 1572864 | tf_op jit(solution)/shard_map/all_gather | solution.py:57
  827.7 11.3 %all-to-all-start.10 = ((f32[16,8,256]{2,1,0:T(8,128)}), f32[16,8,256]{2,1,0:T(8,128)S(1)}, u32[]{:S(2)}, u32[]{:S(2)}) async-start(f32[16,8,256]{2,1,0:T(8,128)} %broadcast_in_dim.129), calls=%async_computation.10 | async-start | bytes 262144 | tf_op jit(solution)/shard_map/all_to_all | solution.py:45
  857.0 11.5 %all-to-all-start.11 = ((f32[16,8,256]{2,1,0:T(8,128)}), f32[16,8,256]{2,1,0:T(8,128)S(1)}, u32[]{:S(2)}, u32[]{:S(2)}) async-start(f32[16,8,256]{2,1,0:T(8,128)} %broadcast_in_dim.130), calls=%async_computation.11 | async-start | bytes 262144 | tf_op jit(solution)/shard_map/all_to_all | solution.py:45
  860.7 76.4 %all-gather.19.cloned.1.call-start = ((), (), s32[]{:S(2)}) async-start(), calls=%async_computation.16 | async-start | bytes 1572864 | tf_op jit(solution)/shard_map/all_gather | solution.py:57
  885.1 38.7 %copy-start.8 = (s32[2]{0:T(128)S(1)}, s32[2]{0:T(128)}, u32[]{:S(2)}) copy-start(s32[2]{0:T(128)} %constant.972.clone.1) | copy-start | bytes 28
  885.2 39.3 %copy-start.7 = (s32[2]{0:T(128)S(1)}, s32[2]{0:T(128)}, u32[]{:S(2)}) copy-start(s32[2]{0:T(128)} %constant.973.clone.1) | copy-start | bytes 28
  885.2 40.1 %copy-start.6 = (s32[2]{0:T(128)S(1)}, s32[2]{0:T(128)}, u32[]{:S(2)}) copy-start(s32[2]{0:T(128)} %constant.974.clone.1) | copy-start | bytes 28
Sparse Core Ops, SparseCore 0:
  233.1 9.6 all-gather.10
  400.9 10.9 all-gather.12
  572.9 10.9 all-gather.14
  746.0 10.9 all-gather.16
  922.6 10.9 all-gather.18
where the time goes:
time: 1040 us; the launch traced here: 1030 us
  blocking collectives  467 us (45%)
  local copies, waits for them, and re-layouts  323 us (31%)
  other arithmetic  97.5 us (9%)
  waiting for transfers between devices  82.3 us (8%)
  starting transfers between devices  31.2 us (3%)
  between operations  30.1 us (3%)
    psum x24, blocking collectives, by_axis(): array = lax.psum(array, axis)  208 us
    all_gather x15, blocking collectives, all_blocks(): parts = lax.all_gather(parts, axes[k], axis=0, tiled=True)  183 us
    gather x10, local copies, waits for them, and re-layouts, local(): precondition_picked = jnp.where(near[None], grouped[:, local_cols], 0.0)  141 us
    gather x5, local copies, waits for them, and re-layouts, local(): picked = whole[:, block_cols]  82.7 us
    all_to_all x7, blocking collectives, copy_for_each(): lax.all_to_all(jnp.broadcast_to(array[None], (length, *array.shape)), axi...  76.5 us
    transpose x5, local copies, waits for them, and re-layouts, all_blocks(): parts.transpose(*turned, *range(len(sequence), parts.ndim))  49.1 us
    unnamed x26, other arithmetic  43.2 us
    all_gather x5, waiting for transfers between devices, all_blocks(): parts = lax.all_gather(parts, axes[k], axis=0, tiled=True)  42.4 us
  transfers between devices with their start and end apart: 13, of which 8 were waited for; matrix products, arithmetic and copies ran while one was open for 3% of the time, Pallas kernels for 0%

commit v1 on v0

--- a/solution.py
+++ b/solution.py
@@ -54,7 +54,9 @@
 def all_blocks(array, axes, sequence):
     parts = array[None]
     for k in sequence:
-        parts = lax.all_gather(parts, axes[k], axis=0, tiled=True)
+        parts = jnp.concatenate(
+            lax.all_to_all(jnp.stack([parts] * lax.axis_size(axes[k])), axes[k], 0, 0), axis=0
+        )
     held = [lax.axis_size(axes[k]) for k in reversed(sequence)]
     parts = parts.reshape(*held, *array.shape)
     turned = sorted(range(len(sequence)), key=lambda place: sequence[len(sequence) - 1 - place])

time: 1040 us -> 937 us (0.901)
  blocking collectives: 467 us -> 372 us
  starting transfers between devices: 31.2 us -> 52.4 us
  waiting for transfers between devices: 82.3 us -> 64.9 us
  between operations: 30.1 us -> 17.2 us
    all_gather x15 -> x0, blocking collectives: 183 us -> none  [all_blocks(): parts = lax.all_gather(parts, axes[k], axis=0, tiled=True)]
    all_to_all x0 -> x14, blocking collectives: none -> 99.5 us  [all_blocks(): lax.all_to_all(jnp.stack([parts] * lax.axis_size(axes[k])), axes[k], 0, 0)]
    transpose x5, local copies, waits for them, and re-layouts: 49.1 us -> 0.63 us  [all_blocks(): parts.transpose(*turned, *range(len(sequence), parts.ndim))]
    all_gather x5 -> x0, waiting for transfers between devices: 42.4 us -> none  [all_blocks(): parts = lax.all_gather(parts, axes[k], axis=0, tiled=True)]
    transpose x10 -> x15, local copies, waits for them, and re-layouts: 5.97 us -> 47.4 us  [in_order(): return jnp.moveaxis(parts, 0, dim).reshape(dims)]
    all_to_all x0 -> x6, waiting for transfers between devices: none -> 25.5 us  [all_blocks(): lax.all_to_all(jnp.stack([parts] * lax.axis_size(axes[k])), axes[k], 0, 0)]
    all_to_all x0 -> x6, starting transfers between devices: none -> 21.5 us  [all_blocks(): lax.all_to_all(jnp.stack([parts] * lax.axis_size(axes[k])), axes[k], 0, 0)]
    psum x24, blocking collectives: 208 us -> 196 us  [by_axis(): array = lax.psum(array, axis)]
  transfers between devices with their start and end apart: 13 -> 14, of which waited for: 8 -> 10; matrix products, arithmetic and copies ran while one was open for 3% -> 3% of each run, Pallas kernels for 0% -> 0%
where the time goes in v1:
time: 937 us; the launch traced here: 925 us
  blocking collectives  372 us (40%)
  local copies, waits for them, and re-layouts  321 us (34%)
  other arithmetic  97.5 us (10%)
  waiting for transfers between devices  64.9 us (7%)
  starting transfers between devices  52.4 us (6%)
  between operations  17.2 us (2%)
    psum x24, blocking collectives, by_axis(): array = lax.psum(array, axis)  196 us
    gather x10, local copies, waits for them, and re-layouts, local(): precondition_picked = jnp.where(near[None], grouped[:, local_cols], 0.0)  141 us
    all_to_all x14, blocking collectives, all_blocks(): lax.all_to_all(jnp.stack([parts] * lax.axis_size(axes[k])), axes[k], 0, 0)  99.5 us
    gather x5, local copies, waits for them, and re-layouts, local(): picked = whole[:, block_cols]  82.7 us
    all_to_all x7, blocking collectives, copy_for_each(): lax.all_to_all(jnp.broadcast_to(array[None], (length, *array.shape)), axi...  76.3 us
    transpose x15, local copies, waits for them, and re-layouts, in_order(): return jnp.moveaxis(parts, 0, dim).reshape(dims)  47.4 us
    unnamed x26, other arithmetic  43.2 us
    all_to_all x6, waiting for transfers between devices, all_blocks(): lax.all_to_all(jnp.stack([parts] * lax.axis_size(axes[k])), axes[k], 0, 0)  25.5 us
  transfers between devices with their start and end apart: 14, of which 10 were waited for; matrix products, arithmetic and copies ran while one was open for 3% of the time, Pallas kernels for 0%

profile of v1, /device:TPU:2, one launch (start us, length us, event | category | flops | bytes accessed | tf_op | source)
XLA Modules:
  0.0 924.9 jit_solution(3027230983793422690)
XLA Ops:
  11.5 8.8 all-to-all-start
  21.8 9.4 %psum.308 = f32[]{:T(128)} all-reduce(f32[]{:T(128)} %multiply_reduce_fusion.31), channel_id=1, replica_groups=mesh['grp_0'=4,'grp_1'=2,'blk_0'=4,'blk_1'=4] {'grp_0'}, use_global_device_ids=true, to_apply=%region_1.2 | all-reduce | flops 1 | bytes 8 | tf_op jit(solution)/shard_map/psum | solution.py:72
  37.1 10.9 %psum.310 = f32[]{:T(128)} all-reduce(f32[]{:T(128)} %psum.309), channel_id=1, replica_groups=mesh['grp_0'=4,'grp_1'=2,'blk_0'=4,'blk_1'=4] {'blk_0'}, use_global_device_ids=true, to_apply=%region_3.4 | all-reduce | flops 1 | bytes 8 | tf_op jit(solution)/shard_map/psum | solution.py:72
  50.3 11.8 %psum.311 = f32[]{:T(128)} all-reduce(f32[]{:T(128)} %psum.310), channel_id=1, replica_groups=mesh['grp_0'=4,'grp_1'=2,'blk_0'=4,'blk_1'=4] {'blk_1'}, use_global_device_ids=true, to_apply=%region_4.5 | all-reduce | flops 1 | bytes 8 | tf_op jit(solution)/shard_map/psum | solution.py:72
  71.3 17.9 %all-to-all-done.1 = f32[128,1,2048]{2,1,0:T(1,128)S(1)} async-done(((f32[128,1,2048]{2,1,0:T(1,128)}), f32[128,1,2048]{2,1,0:T(1,128)S(1)}, u32[]{:S(2)}, u32[]{:S(2)}) %all-to-all-start.1) | async-done | bytes 1048608 | tf_op jit(solution)/shard_map/all_to_all | solution.py:137
  96.3 23.6 %scatter_custom_fusion.1 = f32[4096,64]{1,0:T(8,128)S(1)} fusion(s32[4096]{0:T(1024)S(1)} %reshape.1995, f32[4096,64]{1,0:T(8,128)} %bitcast.649, f32[]{:T(128)} %constant.944.clone.1), kind=kCustom, calls=%fused_computation.48 | custom fusion | flops 262144 | bytes 1049088
  119.9 9.9 %scatter_fusion = f32[16,64,256]{1,2,0:T(8,128)S(1)} fusion(f32[16,64,256]{1,2,0:T(8,128)S(1)} %bitcast.606, s32[192]{0:T(256)S(1)} %reshape.1989, f32[192,64]{1,0:T(8,128)S(1)} %bitcast.671), kind=kCustom, calls=%fused_computation.15 | custom fusion | flops 12288 | bytes 148992 | tf_op jit(solution)/shard_map/scatter-add | solution.py:125
  144.2 14.1 %gather_fusion = f32[4096,8]{1,0:T(8,128)} fusion(f32[8,4096]{0,1:T(8,128)S(1)} %bitcast.609, s32[4096]{0:T(1024)S(1)} %broadcast_clamp_fusion.1), kind=kCustom, calls=%fused_computation | custom fusion | bytes 278528 | tf_op jit(solution)/shard_map/gather | solution.py:182
  161.0 11.3 %all_to_all.171 = f32[16,8,256]{2,1,0:T(8,128)S(1)} all-to-all(f32[16,8,256]{2,1,0:T(8,128)S(1)} %broadcast_in_dim.107), channel_id=1, replica_groups=mesh['grp_0'=4,'grp_1'=2,'blk_0'=4,'blk_1'=4] {'blk_0','blk_1'}, dimensions={0} | all-to-all | bytes 262144 | tf_op jit(solution)/shard_map/all_to_all | solution.py:45
  172.8 14.1 %gather_fusion.1 = f32[4096,8]{1,0:T(8,128)} fusion(f32[8,4096]{0,1:T(8,128)S(1)} %bitcast.610, s32[4096]{0:T(1024)S(1)} %broadcast_clamp_fusion.1), kind=kCustom, calls=%fused_computation.1 | custom fusion | bytes 278528 | tf_op jit(solution)/shard_map/gather | solution.py:182
  197.3 8.4 all_to_all.173
  231.1 16.5 %gather_fusion.2 = f32[4096,8]{1,0:T(8,128)S(1)} fusion(f32[8,32768]{0,1:T(8,128)} %bitcast.602, s32[4096]{0:T(1024)S(1)} %broadcast_clamp_fusion), kind=kCustom, calls=%fused_computation.2 | custom fusion | bytes 278528 | tf_op jit(solution)/shard_map/gather | solution.py:188
  248.9 9.8 %all-reduce.15 = (f32[1]{0:T(128)}, f32[]{:T(128)}) all-reduce(f32[1]{0:T(128)} %bitcast.134, f32[]{:T(128)} %get-tuple-element.441), channel_id=1, replica_groups=mesh['grp_0'=4,'grp_1'=2,'blk_0'=4,'blk_1'=4] {'grp_0'}, use_global_device_ids=true, to_apply=%region_8.9 | all-reduce | flops 2 | bytes 16 | tf_op jit(solution)/shard_map/psum | solution.py:72
  261.8 9.5 %all-reduce.10 = (f32[1]{0:T(128)}, f32[]{:T(128)}) all-reduce(f32[1]{0:T(128)} %get-tuple-element.481, f32[]{:T(128)} %get-tuple-element.482), channel_id=1, replica_groups=mesh['grp_0'=4,'grp_1'=2,'blk_0'=4,'blk_1'=4] {'blk_0'}, use_global_device_ids=true, to_apply=%region_10.11 | all-reduce | flops 2 | bytes 16 | tf_op jit(solution)/shard_map/psum | solution.py:72
  271.3 9.5 %all-reduce.5 = (f32[1]{0:T(128)}, f32[]{:T(128)}) all-reduce(f32[1]{0:T(128)} %get-tuple-element.461, f32[]{:T(128)} %get-tuple-element.462), channel_id=1, replica_groups=mesh['grp_0'=4,'grp_1'=2,'blk_0'=4,'blk_1'=4] {'blk_1'}, use_global_device_ids=true, to_apply=%region_11.12 | all-reduce | flops 2 | bytes 16 | tf_op jit(solution)/shard_map/psum | solution.py:72
  283.5 10.4 %all_to_all.175 = f32[16,8,256]{2,1,0:T(8,128)S(1)} all-to-all(f32[16,8,256]{2,1,0:T(8,128)S(1)} %broadcast_in_dim.109), channel_id=1, replica_groups=mesh['grp_0'=4,'grp_1'=2,'blk_0'=4,'blk_1'=4] {'blk_0','blk_1'}, dimensions={0} | all-to-all | bytes 262144 | tf_op jit(solution)/shard_map/all_to_all | solution.py:45
  294.5 14.1 %gather_fusion.3 = f32[4096,8]{1,0:T(8,128)} fusion(f32[8,4096]{0,1:T(8,128)S(1)} %bitcast.611, s32[4096]{0:T(1024)S(1)} %broadcast_clamp_fusion.1), kind=kCustom, calls=%fused_computation.3 | custom fusion | bytes 278528 | tf_op jit(solution)/shard_map/gather | solution.py:182
  311.3 11.3 %all_to_all.176 = f32[16,8,256]{2,1,0:T(8,128)S(1)} all-to-all(f32[16,8,256]{2,1,0:T(8,128)S(1)} %broadcast_in_dim.110), channel_id=1, replica_groups=mesh['grp_0'=4,'grp_1'=2,'blk_0'=4,'blk_1'=4] {'blk_0','blk_1'}, dimensions={0} | all-to-all | bytes 262144 | tf_op jit(solution)/shard_map/all_to_all | solution.py:45
  323.2 14.1 %gather_fusion.4 = f32[4096,8]{1,0:T(8,128)} fusion(f32[8,4096]{0,1:T(8,128)S(1)} %bitcast.612, s32[4096]{0:T(1024)S(1)} %broadcast_clamp_fusion.1), kind=kCustom, calls=%fused_computation.4 | custom fusion | bytes 278528 | tf_op jit(solution)/shard_map/gather | solution.py:182
  347.5 8.4 all_to_all.178
  355.9 10.7 %all_to_all.179 = f32[4,16,8,256]{3,2,1,0:T(8,128)S(1)} all-to-all(f32[4,16,8,256]{3,2,1,0:T(8,128)S(1)} %stack.169), channel_id=1, replica_groups=mesh['grp_0'=4,'grp_1'=2,'blk_0'=4,'blk_1'=4] {'blk_1'}, dimensions={0} | all-to-all | bytes 1048576 | tf_op jit(solution)/shard_map/all_to_all | solution.py:58
  379.6 16.5 %gather_fusion.5 = f32[4096,8]{1,0:T(8,128)S(1)} fusion(f32[8,32768]{0,1:T(8,128)} %bitcast.603, s32[4096]{0:T(1024)S(1)} %broadcast_clamp_fusion), kind=kCustom, calls=%fused_computation.5 | custom fusion | bytes 278528 | tf_op jit(solution)/shard_map/gather | solution.py:188
  398.8 9.8 %all-reduce.14 = (f32[2]{0:T(128)S(1)}, f32[]{:T(128)}) all-reduce(f32[2]{0:T(128)S(1)} %pad_maximum_fusion.5, f32[]{:T(128)} %get-tuple-element.438), channel_id=1, replica_groups=mesh['grp_0'=4,'grp_1'=2,'blk_0'=4,'blk_1'=4] {'grp_0'}, use_global_device_ids=true, to_apply=%region_20.21 | all-reduce | flops 3 | bytes 24 | tf_op jit(solution)/shard_map/psum | solution.py:72
  411.7 9.5 %all-reduce.9 = (f32[2]{0:T(128)S(1)}, f32[]{:T(128)}) all-reduce(f32[2]{0:T(128)S(1)} %get-tuple-element.479, f32[]{:T(128)} %get-tuple-element.480), channel_id=1, replica_groups=mesh['grp_0'=4,'grp_1'=2,'blk_0'=4,'blk_1'=4] {'blk_0'}, use_global_device_ids=true, to_apply=%region_22.23 | all-reduce | flops 3 | bytes 24 | tf_op jit(solution)/shard_map/psum | solution.py:72
  421.2 9.8 %all-reduce.4 = (f32[2]{0:T(128)S(1)}, f32[]{:T(128)}) all-reduce(f32[2]{0:T(128)S(1)} %get-tuple-element.459, f32[]{:T(128)} %get-tuple-element.460), channel_id=1, replica_groups=mesh['grp_0'=4,'grp_1'=2,'blk_0'=4,'blk_1'=4] {'blk_1'}, use_global_device_ids=true, to_apply=%region_23.24 | all-reduce | flops 3 | bytes 24 | tf_op jit(solution)/shard_map/psum | solution.py:72
  434.9 10.4 %all_to_all.181 = f32[16,8,256]{2,1,0:T(8,128)S(1)} all-to-all(f32[16,8,256]{2,1,0:T(8,128)S(1)} %broadcast_in_dim.111), channel_id=1, replica_groups=mesh['grp_0'=4,'grp_1'=2,'blk_0'=4,'blk_1'=4] {'blk_0','blk_1'}, dimensions={0} | all-to-all | bytes 262144 | tf_op jit(solution)/shard_map/all_to_all | solution.py:45
  445.9 14.1 %gather_fusion.6 = f32[4096,8]{1,0:T(8,128)} fusion(f32[8,4096]{0,1:T(8,128)S(1)} %bitcast.613, s32[4096]{0:T(1024)S(1)} %broadcast_clamp_fusion.1), kind=kCustom, calls=%fused_computation.6 | custom fusion | bytes 278528 | tf_op jit(solution)/shard_map/gather | solution.py:182
  462.7 11.3 %all_to_all.182 = f32[16,8,256]{2,1,0:T(8,128)S(1)} all-to-all(f32[16,8,256]{2,1,0:T(8,128)S(1)} %broadcast_in_dim.112), channel_id=1, replica_groups=mesh['grp_0'=4,'grp_1'=2,'blk_0'=4,'blk_1'=4] {'blk_0','blk_1'}, dimensions={0} | all-to-all | bytes 262144 | tf_op jit(solution)/shard_map/all_to_all | solution.py:45
  474.5 14.1 %gather_fusion.7 = f32[4096,8]{1,0:T(8,128)} fusion(f32[8,4096]{0,1:T(8,128)S(1)} %bitcast.614, s32[4096]{0:T(1024)S(1)} %broadcast_clamp_fusion.1), kind=kCustom, calls=%fused_computation.7 | custom fusion | bytes 278528 | tf_op jit(solution)/shard_map/gather | solution.py:182
  507.2 10.7 %all_to_all.185 = f32[4,16,8,256]{3,2,1,0:T(8,128)S(1)} all-to-all(f32[4,16,8,256]{3,2,1,0:T(8,128)S(1)} %stack.176), channel_id=1, replica_groups=mesh['grp_0'=4,'grp_1'=2,'blk_0'=4,'blk_1'=4] {'blk_1'}, dimensions={0} | all-to-all | bytes 1048576 | tf_op jit(solution)/shard_map/all_to_all | solution.py:58
  531.0 16.5 %gather_fusion.8 = f32[4096,8]{1,0:T(8,128)S(1)} fusion(f32[8,32768]{0,1:T(8,128)} %bitcast.604, s32[4096]{0:T(1024)S(1)} %broadcast_clamp_fusion), kind=kCustom, calls=%fused_computation.8 | custom fusion | bytes 278528 | tf_op jit(solution)/shard_map/gather | solution.py:188
  550.8 9.8 %all-reduce.13 = (f32[3]{0:T(128)S(1)}, f32[]{:T(128)}) all-reduce(f32[3]{0:T(128)S(1)} %pad_maximum_fusion.6, f32[]{:T(128)} %get-tuple-element.434), channel_id=1, replica_groups=mesh['grp_0'=4,'grp_1'=2,'blk_0'=4,'blk_1'=4] {'grp_0'}, use_global_device_ids=true, to_apply=%region_34.35 | all-reduce | flops 4 | bytes 32 | tf_op jit(solution)/shard_map/psum | solution.py:72
  563.7 9.5 %all-reduce.8 = (f32[3]{0:T(128)S(1)}, f32[]{:T(128)}) all-reduce(f32[3]{0:T(128)S(1)} %get-tuple-element.477, f32[]{:T(128)} %get-tuple-element.478), channel_id=1, replica_groups=mesh['grp_0'=4,'grp_1'=2,'blk_0'=4,'blk_1'=4] {'blk_0'}, use_global_device_ids=true, to_apply=%region_36.37 | all-reduce | flops 4 | bytes 32 | tf_op jit(solution)/shard_map/psum | solution.py:72
  573.2 9.6 %all-reduce.3 = (f32[3]{0:T(128)S(1)}, f32[]{:T(128)}) all-reduce(f32[3]{0:T(128)S(1)} %get-tuple-element.457, f32[]{:T(128)} %get-tuple-element.458), channel_id=1, replica_groups=mesh['grp_0'=4,'grp_1'=2,'blk_0'=4,'blk_1'=4] {'blk_1'}, use_global_device_ids=true, to_apply=%region_37.38 | all-reduce | flops 4 | bytes 32 | tf_op jit(solution)/shard_map/psum | solution.py:72
  587.3 10.4 %all_to_all.187 = f32[16,8,256]{2,1,0:T(8,128)S(1)} all-to-all(f32[16,8,256]{2,1,0:T(8,128)S(1)} %broadcast_in_dim.113), channel_id=1, replica_groups=mesh['grp_0'=4,'grp_1'=2,'blk_0'=4,'blk_1'=4] {'blk_0','blk_1'}, dimensions={0} | all-to-all | bytes 262144 | tf_op jit(solution)/shard_map/all_to_all | solution.py:45
  598.3 14.1 %gather_fusion.9 = f32[4096,8]{1,0:T(8,128)} fusion(f32[8,4096]{0,1:T(8,128)S(1)} %bitcast.615, s32[4096]{0:T(1024)S(1)} %broadcast_clamp_fusion.1), kind=kCustom, calls=%fused_computation.9 | custom fusion | bytes 278528 | tf_op jit(solution)/shard_map/gather | solution.py:182
  615.1 11.3 %all_to_all.188 = f32[16,8,256]{2,1,0:T(8,128)S(1)} all-to-all(f32[16,8,256]{2,1,0:T(8,128)S(1)} %broadcast_in_dim.114), channel_id=1, replica_groups=mesh['grp_0'=4,'grp_1'=2,'blk_0'=4,'blk_1'=4] {'blk_0','blk_1'}, dimensions={0} | all-to-all | bytes 262144 | tf_op jit(solution)/shard_map/all_to_all | solution.py:45
  627.0 14.1 %gather_fusion.10 = f32[4096,8]{1,0:T(8,128)} fusion(f32[8,4096]{0,1:T(8,128)S(1)} %bitcast.616, s32[4096]{0:T(1024)S(1)} %broadcast_clamp_fusion.1), kind=kCustom, calls=%fused_computation.10 | custom fusion | bytes 278528 | tf_op jit(solution)/shard_map/gather | solution.py:182
  686.6 16.5 %gather_fusion.11 = f32[4096,8]{1,0:T(8,128)S(1)} fusion(f32[8,32768]{0,1:T(8,128)} %bitcast.605, s32[4096]{0:T(1024)S(1)} %broadcast_clamp_fusion), kind=kCustom, calls=%fused_computation.11 | custom fusion | bytes 278528 | tf_op jit(solution)/shard_map/gather | solution.py:188
  707.0 9.8 %all-reduce.12 = (f32[4]{0:T(128)S(1)}, f32[]{:T(128)}) all-reduce(f32[4]{0:T(128)S(1)} %pad_maximum_fusion.7, f32[]{:T(128)} %get-tuple-element.429), channel_id=1, replica_groups=mesh['grp_0'=4,'grp_1'=2,'blk_0'=4,'blk_1'=4] {'grp_0'}, use_global_device_ids=true, to_apply=%region_49.50 | all-reduce | flops 5 | bytes 40 | tf_op jit(solution)/shard_map/psum | solution.py:72
  720.0 9.5 %all-reduce.7 = (f32[4]{0:T(128)S(1)}, f32[]{:T(128)}) all-reduce(f32[4]{0:T(128)S(1)} %get-tuple-element.475, f32[]{:T(128)} %get-tuple-element.476), channel_id=1, replica_groups=mesh['grp_0'=4,'grp_1'=2,'blk_0'=4,'blk_1'=4] {'blk_0'}, use_global_device_ids=true, to_apply=%region_51.52 | all-reduce | flops 5 | bytes 40 | tf_op jit(solution)/shard_map/psum | solution.py:72
  729.5 9.5 %all-reduce.2 = (f32[4]{0:T(128)S(1)}, f32[]{:T(128)}) all-reduce(f32[4]{0:T(128)S(1)} %get-tuple-element.455, f32[]{:T(128)} %get-tuple-element.456), channel_id=1, replica_groups=mesh['grp_0'=4,'grp_1'=2,'blk_0'=4,'blk_1'=4] {'blk_1'}, use_global_device_ids=true, to_apply=%region_52.53 | all-reduce | flops 5 | bytes 40 | tf_op jit(solution)/shard_map/psum | solution.py:72
  756.8 14.1 %gather_fusion.12 = f32[4096,8]{1,0:T(8,128)} fusion(f32[8,4096]{0,1:T(8,128)S(1)} %bitcast.617, s32[4096]{0:T(1024)S(1)} %broadcast_clamp_fusion.1), kind=kCustom, calls=%fused_computation.12 | custom fusion | bytes 278528 | tf_op jit(solution)/shard_map/gather | solution.py:182
  786.3 14.1 %gather_fusion.13 = f32[4096,8]{1,0:T(8,128)} fusion(f32[8,4096]{0,1:T(8,128)S(1)} %bitcast.608, s32[4096]{0:T(1024)S(1)} %broadcast_clamp_fusion.1), kind=kCustom, calls=%fused_computation.13 | custom fusion | bytes 278528 | tf_op jit(solution)/shard_map/gather | solution.py:182
  847.4 16.5 %gather_fusion.14 = f32[4096,8]{1,0:T(8,128)S(1)} fusion(f32[8,32768]{0,1:T(8,128)} %bitcast.601, s32[4096]{0:T(1024)S(1)} %broadcast_clamp_fusion), kind=kCustom, calls=%fused_computation.14 | custom fusion | bytes 278528 | tf_op jit(solution)/shard_map/gather | solution.py:188
  868.6 9.8 %all-reduce.11 = (f32[5]{0:T(128)S(1)}, f32[]{:T(128)}) all-reduce(f32[5]{0:T(128)S(1)} %stack.200, f32[]{:T(128)} %get-tuple-element.423), channel_id=1, replica_groups=mesh['grp_0'=4,'grp_1'=2,'blk_0'=4,'blk_1'=4] {'grp_0'}, use_global_device_ids=true, to_apply=%region_65.66 | all-reduce | flops 6 | bytes 48 | tf_op jit(solution)/shard_map/psum | solution.py:72
  881.5 9.5 %all-reduce.6 = (f32[5]{0:T(128)S(1)}, f32[]{:T(128)}) all-reduce(f32[5]{0:T(128)S(1)} %get-tuple-element.473, f32[]{:T(128)} %get-tuple-element.474), channel_id=1, replica_groups=mesh['grp_0'=4,'grp_1'=2,'blk_0'=4,'blk_1'=4] {'blk_0'}, use_global_device_ids=true, to_apply=%region_67.68 | all-reduce | flops 6 | bytes 48 | tf_op jit(solution)/shard_map/psum | solution.py:72
  891.0 10.4 %all-reduce.1 = (f32[5]{0:T(128)S(1)}, f32[]{:T(128)}) all-reduce(f32[5]{0:T(128)S(1)} %get-tuple-element.453, f32[]{:T(128)} %get-tuple-element.454), channel_id=1, replica_groups=mesh['grp_0'=4,'grp_1'=2,'blk_0'=4,'blk_1'=4] {'blk_1'}, use_global_device_ids=true, to_apply=%region_68.69 | all-reduce | flops 6 | bytes 48 | tf_op jit(solution)/shard_map/psum | solution.py:72
  (357 shorter events, 332.2 us)
Async XLA Ops:
  2.0 60.9 %collective-permute-start.1 = (s32[1]{0:T(128)}, s32[1]{0:T(128)}, u32[]{:S(2)}, u32[]{:S(2)}) collective-permute-start(s32[1]{0:T(128)} %bitcast.71), channel_id=1, source_target_pairs={{127,0},{0,1},{1,2},{2,3},{3,4},{4,5},{5,6},{6,7},{7,8},{8,9},{9,1... | collective-permute-start | bytes 20 | tf_op jit(solution)/shard_map/ppermute | solution.py:34
  4.8 66.4 %collective-permute-start.2 = (f32[64,96]{1,0:T(8,128)S(1)}, f32[64,96]{1,0:T(8,128)S(1)}, u32[]{:S(2)}, u32[]{:S(2)}) collective-permute-start(f32[64,96]{1,0:T(8,128)S(1)} %slice.984), channel_id=1, source_target_pairs={{127,0},{0,1},{1,2},{2,3},{3,4},{4,5},{5,6},{6,7},{7,8},{8,9},{9,1... | collective-permute-start | bytes 73736 | tf_op jit(solution)/shard_map/ppermute | solution.py:34
  7.5 56.9 %collective-permute-start = (s32[96]{0:T(128)S(1)}, s32[96]{0:T(128)S(1)}, u32[]{:S(2)}, u32[]{:S(2)}) collective-permute-start(s32[96]{0:T(128)S(1)} %slice_bitcast_fusion.6), channel_id=1, source_target_pairs={{127,0},{0,1},{1,2},{2,3},{3,4},{4,5},{5,6},{6,7},{7,8},{8,9},{9,1... | collective-permute-start | bytes 1160 | tf_op jit(solution)/shard_map/ppermute | solution.py:34
  11.5 53.0 %all-to-all-start = ((s32[1,128,33]{2,0,1:T(1,128)}), s32[1,128,33]{2,0,1:T(1,128)S(1)}, u32[]{:S(2)}, u32[]{:S(2)}) async-start(s32[1,128,33]{2,0,1:T(1,128)} %copy.71), calls=%async_computation | async-start | bytes 131072 | tf_op jit(solution)/shard_map/all_to_all | solution.py:20
  37.1 25.7 %copy-start.1 = (f32[8,256]{1,0:T(8,128)S(1)}, f32[8,256]{1,0:T(8,128)}, u32[]{:S(2)}) copy-start(f32[8,256]{1,0:T(8,128)} %param.81) | copy-start | bytes 24580
  37.1 25.8 %copy-start.3 = (s32[16,256]{1,0:T(8,128)S(1)}, s32[16,256]{1,0:T(8,128)}, u32[]{:S(2)}) copy-start(s32[16,256]{1,0:T(8,128)} %param.80) | copy-start | bytes 49156
  50.3 20.3 %copy-start.5 = (s32[2]{0:T(128)S(1)}, s32[2]{0:T(128)}, u32[]{:S(2)}) copy-start(s32[2]{0:T(128)} %constant.981) | copy-start | bytes 28
  50.3 20.4 %copy-start.4 = (s32[2]{0:T(128)S(1)}, s32[2]{0:T(128)}, u32[]{:S(2)}) copy-start(s32[2]{0:T(128)} %constant.984) | copy-start | bytes 28
  64.5 24.8 %all-to-all-start.1 = ((f32[128,1,2048]{2,1,0:T(1,128)}), f32[128,1,2048]{2,1,0:T(1,128)S(1)}, u32[]{:S(2)}, u32[]{:S(2)}) async-start(f32[128,1,2048]{2,1,0:T(1,128)} %reshape.2107), calls=%async_computation.1 | async-start | bytes 2097152 | tf_op jit(solution)/shard_map/all_to_all | solution.py:137
  129.8 0.7 copy-start.2
  130.7 733.8 %copy-start = (f32[16,8,8,256]{3,2,1,0:T(8,128)}, f32[16,8,8,256]{3,2,1,0:T(8,128)S(1)}, u32[]{:S(2)}) copy-start(f32[16,8,8,256]{3,2,1,0:T(8,128)S(1)} %get-tuple-element.493) | copy-start | bytes 3145732
  132.3 11.3 %all-to-all-start.2 = ((f32[16,8,256]{2,1,0:T(8,128)}), f32[16,8,256]{2,1,0:T(8,128)S(1)}, u32[]{:S(2)}, u32[]{:S(2)}) async-start(f32[16,8,256]{2,1,0:T(8,128)} %broadcast_in_dim.104), calls=%async_computation.2 | async-start | bytes 262144 | tf_op jit(solution)/shard_map/all_to_all | solution.py:45
  206.5 11.5 %all-to-all-start.6 = ((f32[4,16,8,256]{3,2,1,0:T(8,128)}), f32[4,16,8,256]{3,2,1,0:T(8,128)S(1)}, u32[]{:S(2)}, u32[]{:S(2)}) async-start(f32[4,16,8,256]{3,2,1,0:T(8,128)} %stack.164), calls=%async_computation.6 | async-start | bytes 1048576 | tf_op jit(solution)/shard_map/all_to_all | solution.py:58
  643.6 23.2 %copy-start.8 = (s32[2]{0:T(128)S(1)}, s32[2]{0:T(128)}, u32[]{:S(2)}) copy-start(s32[2]{0:T(128)} %constant.972.clone.1) | copy-start | bytes 28
  651.9 9.3 %all-to-all-start.23 = ((f32[4,4,8,256]{3,2,1,0:T(8,128)}), f32[4,4,8,256]{3,2,1,0:T(8,128)S(1)}, u32[]{:S(2)}, u32[]{:S(2)}) async-start(f32[4,4,8,256]{3,2,1,0:T(8,128)} %stack.183), calls=%async_computation.23 | async-start | bytes 262144 | tf_op jit(solution)/shard_map/all_to_all | solution.py:58
  662.0 11.5 %all-to-all-start.24 = ((f32[4,16,8,256]{3,2,1,0:T(8,128)}), f32[4,16,8,256]{3,2,1,0:T(8,128)S(1)}, u32[]{:S(2)}, u32[]{:S(2)}) async-start(f32[4,16,8,256]{3,2,1,0:T(8,128)} %stack.184), calls=%async_computation.24 | async-start | bytes 1048576 | tf_op jit(solution)/shard_map/all_to_all | solution.py:58
  703.1 45.9 %copy-start.7 = (s32[2]{0:T(128)S(1)}, s32[2]{0:T(128)}, u32[]{:S(2)}) copy-start(s32[2]{0:T(128)} %constant.973.clone.1) | copy-start | bytes 28
  744.7 11.5 %all-to-all-start.26 = ((f32[16,8,256]{2,1,0:T(8,128)}), f32[16,8,256]{2,1,0:T(8,128)S(1)}, u32[]{:S(2)}, u32[]{:S(2)}) async-start(f32[16,8,256]{2,1,0:T(8,128)} %broadcast_in_dim.115), calls=%async_computation.26 | async-start | bytes 262144 | tf_op jit(solution)/shard_map/all_to_all | solution.py:45
  772.9 5.0 copy-start.6
  774.3 11.5 %all-to-all-start.27 = ((f32[16,8,256]{2,1,0:T(8,128)}), f32[16,8,256]{2,1,0:T(8,128)S(1)}, u32[]{:S(2)}, u32[]{:S(2)}) async-start(f32[16,8,256]{2,1,0:T(8,128)} %broadcast_in_dim.116), calls=%async_computation.27 | async-start | bytes 262144 | tf_op jit(solution)/shard_map/all_to_all | solution.py:45
  803.7 8.4 all-to-all-start.28
  812.8 9.3 %all-to-all-start.29 = ((f32[4,4,8,256]{3,2,1,0:T(8,128)}), f32[4,4,8,256]{3,2,1,0:T(8,128)S(1)}, u32[]{:S(2)}, u32[]{:S(2)}) async-start(f32[4,4,8,256]{3,2,1,0:T(8,128)} %stack.192), calls=%async_computation.29 | async-start | bytes 262144 | tf_op jit(solution)/shard_map/all_to_all | solution.py:58
  822.9 11.5 %all-to-all-start.30 = ((f32[4,16,8,256]{3,2,1,0:T(8,128)}), f32[4,16,8,256]{3,2,1,0:T(8,128)S(1)}, u32[]{:S(2)}, u32[]{:S(2)}) async-start(f32[4,16,8,256]{3,2,1,0:T(8,128)} %stack.193), calls=%async_computation.30 | async-start | bytes 1048576 | tf_op jit(solution)/shard_map/all_to_all | solution.py:58
